TPU v7x, 512 devices: a whole 4x8x8 slice. The times are simulated.
512 devices in a mesh: rows: 8 (over z), cols: 8 (over y), depth: 8 (over x, core).
Axes of the slice: x: 4, y: 8, z: 8, core: 2. Of those that a mesh axis runs over, the one named last changes fastest.
Arguments:
- tokens: bfloat16 [512, 12288], P(('rows', 'cols'), 'depth'), may hold values from -6 to 6
- weight_in: bfloat16 [12288, 49152], P('depth', ('rows', 'cols')), may hold values from -0.0546875 to 0.0546875
- bias_in: float32 [49152], P(('rows', 'cols')), may hold values from -4 to 4
- weight_out: bfloat16 [49152, 12288], P(('rows', 'cols'), 'depth'), may hold values from -0.02734375 to 0.02734375
- bias_out: float32 [12288], P('depth'), may hold values from -3 to 3
Outputs:
- output: bfloat16 [512, 12288], P(('rows', 'cols'), 'depth')
All inputs are finite; a program needn't handle non-finite values.
Results may differ from a plain program's by a relative error of at most 0.0046.
Values may be sent and summed in bfloat16 or wider, within the bound.
No kernel may reach another device: no remote copies, remote signals or barrier semaphores. Data moves between devices by JAX's collectives and lax.ppermute only.
A program may use at most 64 MiB of HBM per device.

v0:
```python
import jax
import jax.numpy as jnp
from jax import lax
from jax.sharding import PartitionSpec as P

PLANE = ("rows", "cols")


def shards(tokens, weight_in, bias_in, weight_out, bias_out):
    own = tokens.shape[0]
    planes = lax.axis_size(PLANE)
    gathered = lax.all_to_all(
        jnp.broadcast_to(tokens[None], (planes,) + tokens.shape), PLANE, 0, 0
    ).reshape(planes * own, -1)
    partial_hidden = jnp.dot(gathered, weight_in, preferred_element_type=jnp.float32)
    depths = lax.axis_size("depth")
    pieces = lax.all_to_all(
        partial_hidden.astype(jnp.bfloat16).reshape(depths, -1, weight_in.shape[1]), "depth", 0, 0
    )
    hidden = jnp.sum(pieces.astype(jnp.float32), axis=0) + bias_in
    active = jax.nn.gelu(hidden, approximate=True).astype(jnp.bfloat16)
    active = lax.all_gather(active, "depth", axis=0, tiled=True)
    partial_out = jnp.dot(active, weight_out, preferred_element_type=jnp.float32)
    parts = lax.all_to_all(partial_out.astype(jnp.bfloat16).reshape(planes, own, -1), PLANE, 0, 0)
    summed = jnp.sum(parts.astype(jnp.float32), axis=0)
    return (summed + bias_out).astype(jnp.bfloat16)


def solution(mesh):
    in_specs = (
        P(("rows", "cols"), "depth"),
        P("depth", ("rows", "cols")),
        P(("rows", "cols")),
        P(("rows", "cols"), "depth"),
        P("depth"),
    )
    out_specs = P(("rows", "cols"), "depth")
    return jax.shard_map(shards, mesh=mesh, in_specs=in_specs, out_specs=out_specs, check_vma=False)
```

profile of v0, /device:TPU:8, one launch (start us, length us, event | category | flops | bytes accessed | tf_op | source)
XLA Modules:
  0.0 142.8 jit_solution(7724320758658860799)
XLA Ops:
  0.0 0.0 copy-start
  0.0 1.0 broadcast_in_dim.2
  1.0 0.0 copy-start.3
  1.0 57.3 %all_to_all.15 = bf16[64,8,1536]{2,1,0:T(8,128)(2,1)S(1)} all-to-all(bf16[64,8,1536]{2,1,0:T(8,128)(2,1)S(1)} %broadcast_in_dim.2), channel_id=1, replica_groups=mesh['rows'=8,'cols'=8,'depth'=8] {'rows','cols'}, dimensions={0} | all-to-all | bytes 3145728 | tf_op jit(solution)/shard_map/all_to_all | solution.py:12
  58.3 0.0 copy-done.3
  58.3 1.4 fusion.3
  59.7 0.0 copy-start.2
  59.7 17.3 %all_to_all.16 = bf16[8,64,768]{2,1,0:T(8,128)(2,1)S(1)} all-to-all(bf16[8,64,768]{2,1,0:T(8,128)(2,1)S(1)} %bitcast.11), channel_id=1, replica_groups=mesh['rows'=8,'cols'=8,'depth'=8] {'depth'}, dimensions={0} | all-to-all | bytes 1572864 | tf_op jit(solution)/shard_map/all_to_all | solution.py:17
  77.0 0.1 convert_reduce_fusion.1
  77.1 0.0 copy-done.2
  77.1 0.1 fusion.13
  77.2 13.5 %all_gather.3 = bf16[512,768]{1,0:T(8,128)(2,1)S(1)} all-gather(bf16[64,768]{1,0:T(8,128)(2,1)S(1)} %fusion.13), channel_id=1, replica_groups=mesh['rows'=8,'cols'=8,'depth'=8] {'depth'}, dimensions={0}, use_global_device_ids=true | all-gather | bytes 884736 | tf_op jit(solution)/shard_map/all_gather | solution.py:22
  90.7 0.0 copy-done
  90.7 1.4 fusion
  92.1 49.4 %all_to_all.17 = bf16[64,8,1536]{2,1,0:T(8,128)(2,1)S(1)} all-to-all(bf16[64,8,1536]{2,1,0:T(8,128)(2,1)S(1)} %fusion), channel_id=1, replica_groups=mesh['rows'=8,'cols'=8,'depth'=8] {'rows','cols'}, dimensions={0} | all-to-all | bytes 3145728 | tf_op jit(solution)/shard_map/all_to_all | solution.py:24
  141.5 0.0 copy-start.1
  141.5 0.2 convert_reduce_fusion
  141.8 0.4 copy-done.1
  142.2 0.6 add_convert_fusion
Async XLA Ops:
  0.0 90.7 %copy-start = (bf16[768,1536]{1,0:T(8,128)(2,1)S(1)}, bf16[768,1536]{1,0:T(8,128)(2,1)}, u32[]{:S(2)}) copy-start(bf16[768,1536]{1,0:T(8,128)(2,1)} %param.8) | copy-start | bytes 7077892
  1.0 57.3 %copy-start.3 = (bf16[1536,768]{1,0:T(8,128)(2,1)S(1)}, bf16[1536,768]{1,0:T(8,128)(2,1)}, u32[]{:S(2)}) copy-start(bf16[1536,768]{1,0:T(8,128)(2,1)} %param.6) | copy-start | bytes 7077892
  59.7 17.5 %copy-start.2 = (f32[768]{0:T(1024)S(1)}, f32[768]{0:T(1024)}, u32[]{:S(2)}) copy-start(f32[768]{0:T(1024)} %param.7) | copy-start | bytes 9220
  141.5 0.7 copy-start.1
where the time goes:
time: 143 us
  blocking collectives  138 us (97%)
  matrix products  2.76 us (2%)
  local copies, waits for them, and re-layouts  1.45 us (1%)
    all_to_all x1, blocking collectives, shards(): lax.all_to_all(jnp.broadcast_to(tokens[None], (planes,) + tokens.shape),...  57.3 us
    all_to_all x1, blocking collectives, shards(): lax.all_to_all(partial_out.astype(jnp.bfloat16).reshape(planes, own, -1),...  49.4 us
    all_to_all x1, blocking collectives, shards(): lax.all_to_all(partial_hidden.astype(jnp.bfloat16).reshape(depths, -1, we...  17.3 us
    all_gather x1, blocking collectives, shards(): active = lax.all_gather(active, 'depth', axis=0, tiled=True)  13.5 us

commit v1 on v0

--- a/solution.py
+++ b/solution.py
@@ -19,7 +19,15 @@
     )
     hidden = jnp.sum(pieces.astype(jnp.float32), axis=0) + bias_in
     active = jax.nn.gelu(hidden, approximate=True).astype(jnp.bfloat16)
-    active = lax.all_gather(active, "depth", axis=0, tiled=True)
+    active = jnp.concatenate(
+        lax.all_to_all(
+            jnp.stack(lax.axis_size("depth") * [active], 0),
+            axis_name="depth",
+            split_axis=0,
+            concat_axis=0,
+        ),
+        axis=0,
+    )
     partial_out = jnp.dot(active, weight_out, preferred_element_type=jnp.float32)
     parts = lax.all_to_all(partial_out.astype(jnp.bfloat16).reshape(planes, own, -1), PLANE, 0, 0)
     summed = jnp.sum(parts.astype(jnp.float32), axis=0)

time: 143 us -> 144 us (level)
    all_to_all x0 -> x1, blocking collectives: none -> 15.7 us  [shards(): lax.all_to_all(jnp.stack(lax.axis_size('depth') * [active], 0), axis_name...]
    all_gather x1 -> x0, blocking collectives: 13.5 us -> none  [shards(): active = lax.all_gather(active, 'depth', axis=0, tiled=True)]
where the time goes in v1:
time: 144 us
  blocking collectives  139 us (97%)
  matrix products  2.76 us (2%)
  local copies, waits for them, and re-layouts  1.5 us (1%)
    all_to_all x1, blocking collectives, shards(): lax.all_to_all(jnp.broadcast_to(tokens[None], (planes,) + tokens.shape),...  57.3 us
    all_to_all x1, blocking collectives, shards(): lax.all_to_all(partial_out.astype(jnp.bfloat16).reshape(planes, own, -1),...  48.5 us
    all_to_all x1, blocking collectives, shards(): lax.all_to_all(partial_hidden.astype(jnp.bfloat16).reshape(depths, -1, we...  17.3 us
    all_to_all x1, blocking collectives, shards(): lax.all_to_all(jnp.stack(lax.axis_size('depth') * [active], 0), axis_name...  15.7 us

profile of v1, /device:TPU:8, one launch (start us, length us, event | category | flops | bytes accessed | tf_op | source)
XLA Modules:
  0.0 144.1 jit_solution(8502085206370971451)
XLA Ops:
  0.0 0.0 copy-start
  0.0 1.0 broadcast_in_dim.2
  1.0 0.0 copy-start.3
  1.0 57.3 %all_to_all.20 = bf16[64,8,1536]{2,1,0:T(8,128)(2,1)S(1)} all-to-all(bf16[64,8,1536]{2,1,0:T(8,128)(2,1)S(1)} %broadcast_in_dim.2), channel_id=1, replica_groups=mesh['rows'=8,'cols'=8,'depth'=8] {'rows','cols'}, dimensions={0} | all-to-all | bytes 3145728 | tf_op jit(solution)/shard_map/all_to_all | solution.py:12
  58.3 0.0 copy-done.3
  58.3 1.4 fusion.3
  59.7 0.0 copy-start.2
  59.7 17.3 %all_to_all.21 = bf16[8,64,768]{2,1,0:T(8,128)(2,1)S(1)} all-to-all(bf16[8,64,768]{2,1,0:T(8,128)(2,1)S(1)} %bitcast.12), channel_id=1, replica_groups=mesh['rows'=8,'cols'=8,'depth'=8] {'depth'}, dimensions={0} | all-to-all | bytes 1572864 | tf_op jit(solution)/shard_map/all_to_all | solution.py:17
  77.0 0.1 convert_reduce_fusion.1
  77.1 0.0 copy-done.2
  77.1 0.1 fusion.13
  77.2 0.1 stack.2
  77.3 15.7 %all_to_all.22 = bf16[8,64,768]{2,1,0:T(8,128)(2,1)S(1)} all-to-all(bf16[8,64,768]{2,1,0:T(8,128)(2,1)S(1)} %stack.2), channel_id=1, replica_groups=mesh['rows'=8,'cols'=8,'depth'=8] {'depth'}, dimensions={0} | all-to-all | bytes 1572864 | tf_op jit(solution)/shard_map/all_to_all | solution.py:23
  92.9 0.0 copy-done
  92.9 1.4 fusion
  94.3 48.5 %all_to_all.23 = bf16[64,8,1536]{2,1,0:T(8,128)(2,1)S(1)} all-to-all(bf16[64,8,1536]{2,1,0:T(8,128)(2,1)S(1)} %fusion), channel_id=1, replica_groups=mesh['rows'=8,'cols'=8,'depth'=8] {'rows','cols'}, dimensions={0} | all-to-all | bytes 3145728 | tf_op jit(solution)/shard_map/all_to_all | solution.py:32
  142.8 0.0 copy-start.1
  142.8 0.2 convert_reduce_fusion
  143.1 0.4 copy-done.1
  143.5 0.6 add_convert_fusion
Async XLA Ops:
  0.0 92.9 %copy-start = (bf16[768,1536]{1,0:T(8,128)(2,1)S(1)}, bf16[768,1536]{1,0:T(8,128)(2,1)}, u32[]{:S(2)}) copy-start(bf16[768,1536]{1,0:T(8,128)(2,1)} %param.8) | copy-start | bytes 7077892
  1.0 57.3 %copy-start.3 = (bf16[1536,768]{1,0:T(8,128)(2,1)S(1)}, bf16[1536,768]{1,0:T(8,128)(2,1)}, u32[]{:S(2)}) copy-start(bf16[1536,768]{1,0:T(8,128)(2,1)} %param.6) | copy-start | bytes 7077892
  59.7 17.5 %copy-start.2 = (f32[768]{0:T(1024)S(1)}, f32[768]{0:T(1024)}, u32[]{:S(2)}) copy-start(f32[768]{0:T(1024)} %param.7) | copy-start | bytes 9220
  142.8 0.7 copy-start.1
